TPU v7x, 256 devices: a whole 4x4x8 slice. The times are simulated.
256 devices in a mesh: row: 8 (over x, y_hi), col: 32 (over y_lo, z, core).
Axes of the slice: x: 4, y: 4 (y_hi: 2, y_lo: 2; y = y_hi * 2 + y_lo), z: 8, core: 2. Of those that a mesh axis runs over, the one named last changes fastest.
Arguments:
- queries: bfloat16 [32768, 1024], P(('row', 'col'))
- keys: bfloat16 [32768, 128], P(('row', 'col'))
- values: bfloat16 [32768, 128], P(('row', 'col')), may hold values from -6 to 6
- positions: int32 [32768], P(('row', 'col')), may hold values from 0 to 32767, each once
Outputs:
- attended: bfloat16 [32768, 1024], P(('row', 'col'))
- log_total: float32 [8, 32768], P(None, ('row', 'col'))
Inputs may be any that keep to these rules, and one draw needn't show every extreme that they name: positions is a permutation of 0 to 32767.
All inputs are finite; a program needn't handle non-finite values.
Results may differ from a plain program's by a relative error of at most 0.015.
Values may be sent and summed in bfloat16 or wider, within the bound.
A program may use at most 64 MiB of HBM per device.

v0:
```python
import math

import jax
import jax.numpy as jnp
from jax import lax
from jax.sharding import PartitionSpec as P

HEADS = 8
HD = 128
STEPS = 4


MASKED_SCORE = -1e30


def from_behind(block, axis, distance):
    devices = range(lax.axis_size(axis))
    route = [((i - distance) % len(devices), i) for i in devices]
    return lax.ppermute(block, axis, route)


def for_sending(value):

    def short(part):
        return part.astype(jnp.bfloat16) if part.dtype == jnp.float32 else part

    return jax.tree.map(short, value)


def tile_update(carried, query_heads, query_place, key_block, value_block, key_place):
    accumulated, running_max, weight_total = carried
    scores = jnp.einsum(
        "thd,kd->htk", query_heads, key_block, preferred_element_type=jnp.float32
    ) * HD ** (-0.5)
    visible = key_place[None, :] <= query_place[:, None]
    scores = jnp.where(visible[None], scores, MASKED_SCORE)
    raised = jnp.maximum(running_max, jnp.max(scores, axis=-1))
    rescale = jnp.exp(running_max - raised)
    weights = jnp.where(visible[None], jnp.exp(scores - raised[..., None]), 0.0)
    weight_total = weight_total * rescale + jnp.sum(weights, axis=-1)
    product = jnp.einsum(
        "htk,kd->htd", weights.astype(jnp.bfloat16), value_block, preferred_element_type=jnp.float32
    )
    accumulated = accumulated * rescale[..., None] + product
    return (accumulated, raised, weight_total)


def absorb(carried, query_rows, query_place, key_rows, value_rows, key_place):
    query_heads = query_rows.reshape(query_rows.shape[0], HEADS, HD)
    row_count = key_rows.shape[0]
    block_rows = math.gcd(row_count, 256)
    block_count = row_count // block_rows
    blocks = (
        key_rows.reshape(block_count, block_rows, HD),
        value_rows.reshape(block_count, block_rows, HD),
        key_place.reshape(block_count, block_rows),
    )

    def scan_step(inner, block):
        return (tile_update(inner, query_heads, query_place, block[0], block[1], block[2]), None)

    carried, unused = lax.scan(scan_step, carried, blocks)
    return carried


def local(queries, keys, values, positions):
    token_count = queries.shape[0]
    carried = (
        jnp.zeros((HEADS, token_count, HD), jnp.float32),
        jnp.full((HEADS, token_count), MASKED_SCORE, jnp.float32),
        jnp.zeros((HEADS, token_count), jnp.float32),
    )
    group_keys, group_values, group_place = (
        lax.all_gather(keys, "col", axis=0, tiled=True),
        lax.all_gather(values, "col", axis=0, tiled=True),
        lax.all_gather(positions, "col", axis=0, tiled=True),
    )
    query_rows, query_place = (queries, positions)
    for visit in range(STEPS):
        carried = absorb(carried, query_rows, query_place, group_keys, group_values, group_place)
        if visit + 1 < STEPS:
            query_rows, query_place = from_behind((query_rows, query_place), "row", 1)
            carried = from_behind(carried, "row", 1)
    carried = jax.tree.map(
        lambda part, own: part.astype(own.dtype),
        from_behind(for_sending(carried), "row", 1 - STEPS),
        carried,
    )
    accumulated, running_max, weight_total = carried
    output = (
        (accumulated / weight_total[..., None]).transpose(1, 0, 2).reshape(token_count, HEADS * HD)
    )
    return (output.astype(jnp.bfloat16), running_max + jnp.log(weight_total))


def solution(mesh):
    placed = (
        P(("row", "col"), None),
        P(("row", "col"), None),
        P(("row", "col"), None),
        P(("row", "col")),
    )
    return jax.shard_map(
        local,
        mesh=mesh,
        in_specs=placed,
        out_specs=(P(("row", "col"), None), P(None, ("row", "col"))),
        check_vma=False,
    )
```

profile of v0, /device:TPU:6, one launch (start us, length us, event | category | flops | bytes accessed | tf_op | source)
XLA Modules:
  0.0 414.2 jit_solution(4201912937210326341)
XLA Ops:
  9.3 37.0 %all-gather = s32[32,1,128]{2,1,0:T(1,128)S(1)} all-gather(s32[1,1,128]{2,1,0:T(1,128)S(1)} %bitcast.119), channel_id=1, replica_groups=mesh['row'=8,'col'=32] {'col'}, dimensions={0}, use_global_device_ids=true | all-gather | bytes 16896 | tf_op jit(solution)/shard_map/all_gather | solution.py:76
  49.0 27.4 %all-gather.4.cloned.1.call-done = bf16[4096,128]{1,0:T(8,128)(2,1)} async-done(((bf16[128,128]{1,0:T(8,128)(2,1)}), bf16[4096,128]{1,0:T(8,128)(2,1)}) %all-gather.4.cloned.1.call-update) | async-done | bytes 1048592 | tf_op jit(solution)/shard_map/all_gather | solution.py:74
  76.4 65.2 %all-gather.6.cloned.1.call-done = bf16[4096,128]{1,0:T(8,128)(2,1)} async-done(((bf16[128,128]{1,0:T(8,128)(2,1)}), bf16[4096,128]{1,0:T(8,128)(2,1)}) %all-gather.6.cloned.1.call-update) | async-done | bytes 1048592 | tf_op jit(solution)/shard_map/all_gather | solution.py:75
  141.6 46.1 %while.60 = (s32[]{:T(128)}, f32[8,128,128]{2,1,0:T(8,128)S(1)}, f32[8,128]{1,0:T(8,128)S(1)}, f32[8,128]{1,0:T(8,128)S(1)}, s32[16,256]{1,0:T(8,128)S(1)}, /*in...) while((s32[]{:T(128)}, f32[8,128,128]{2,1,0:T(8,128)S(1)}, ...), condition=%wide.region_3.4_spmd.clone, body=%wide.region_0.3_spmd.clone.sunk | while | flops 137008128 | bytes 4788861 | solution.py:62
  187.6 2.8 collective-permute-start
  191.2 2.7 collective-permute-start.1
  194.0 1.7 collective-permute-start.2
  195.7 2.7 collective-permute-start.3
  198.4 11.5 %collective-permute-done.4 = bf16[128,1024]{0,1:T(8,128)(2,1)S(1)} collective-permute-done((bf16[128,1024]{0,1:T(8,128)(2,1)S(1)}, bf16[128,1024]{0,1:T(8,128)(2,1)S(1)}, u32[]{:S(2)}, u32[]{:S(2)}) %collective-permute-start.4) | collective-permute-done | bytes 262176 | tf_op jit(solution)/shard_map/ppermute | solution.py:19
  210.1 46.0 %while.57 = (s32[]{:T(128)}, f32[8,128,128]{2,1,0:T(8,128)S(1)}, f32[8,128]{1,0:T(8,128)S(1)}, f32[8,128]{1,0:T(8,128)S(1)}, s32[16,256]{1,0:T(8,128)S(1)}, /*in...) while((s32[]{:T(128)}, f32[8,128,128]{2,1,0:T(8,128)S(1)}, ...), condition=%wide.region_7.8_spmd, body=%wide.region_4.7_spmd.sunk | while | flops 136873984 | bytes 4788841 | solution.py:62
  211.6 1.3 convolution_add_fusion.8
  256.1 1.9 collective-permute-start.5
  258.1 2.9 collective-permute-start.9
  261.6 2.6 collective-permute-start.7
  264.2 1.8 collective-permute-start.8
  266.0 11.5 %collective-permute-done.9 = bf16[128,1024]{0,1:T(8,128)(2,1)S(1)} collective-permute-done((bf16[128,1024]{0,1:T(8,128)(2,1)S(1)}, bf16[128,1024]{0,1:T(8,128)(2,1)S(1)}, u32[]{:S(2)}, u32[]{:S(2)}) %collective-permute-start.9) | collective-permute-done | bytes 262176 | tf_op jit(solution)/shard_map/ppermute | solution.py:19
  277.7 46.0 %while.58 = (s32[]{:T(128)}, f32[8,128,128]{2,1,0:T(8,128)S(1)}, f32[8,128]{1,0:T(8,128)S(1)}, f32[8,128]{1,0:T(8,128)S(1)}, s32[16,256]{1,0:T(8,128)S(1)}, /*in...) while((s32[]{:T(128)}, f32[8,128,128]{2,1,0:T(8,128)S(1)}, ...), condition=%wide.region_11.12_spmd, body=%wide.region_8.11_spmd.sunk | while | flops 136873984 | bytes 4788841 | solution.py:62
  324.9 5.0 %collective-permute-start.14 = (bf16[128,1024]{0,1:T(8,128)(2,1)S(1)}, bf16[128,1024]{0,1:T(8,128)(2,1)S(1)}, u32[]{:S(2)}, u32[]{:S(2)}) collective-permute-start(bf16[128,1024]{0,1:T(8,128)(2,1)S(1)} %collective-permute-done.9), channel_id=1, source_target_pairs={{224,0},{0,32},{32,64},{64,96},{96,128},{128,160},{160,192},{192,2... | collective-permute-start | bytes 786440 | tf_op jit(solution)/shard_map/ppermute | solution.py:19
  330.0 1.9 collective-permute-start.12
  332.9 11.3 %collective-permute-done.14 = bf16[128,1024]{0,1:T(8,128)(2,1)S(1)} collective-permute-done((bf16[128,1024]{0,1:T(8,128)(2,1)S(1)}, bf16[128,1024]{0,1:T(8,128)(2,1)S(1)}, u32[]{:S(2)}, u32[]{:S(2)}) %collective-permute-start.14) | collective-permute-done | bytes 262176 | tf_op jit(solution)/shard_map/ppermute | solution.py:19
  344.5 46.0 %while.59 = (s32[]{:T(128)}, f32[8,128,128]{2,1,0:T(8,128)S(1)}, f32[8,128]{1,0:T(8,128)S(1)}, f32[8,128]{1,0:T(8,128)S(1)}, s32[16,256]{1,0:T(8,128)S(1)}, /*in...) while((s32[]{:T(128)}, f32[8,128,128]{2,1,0:T(8,128)S(1)}, ...), condition=%wide.region_15.16_spmd, body=%wide.region_12.15_spmd.sunk | while | flops 136873984 | bytes 4788841 | solution.py:62
  391.6 7.1 %collective-permute-start.16 = (bf16[8,128]{1,0:T(8,128)(2,1)S(1)}, bf16[8,128]{1,0:T(8,128)(2,1)S(1)}, u32[]{:S(2)}, u32[]{:S(2)}) collective-permute-start(bf16[8,128]{1,0:T(8,128)(2,1)S(1)} %convert_element_type.41), channel_id=1, source_target_pairs={{96,0},{128,32},{160,64},{192,96},{224,128},{0,160},{32,192},{64,2... | collective-permute-start | bytes 6152 | tf_op jit(solution)/shard_map/ppermute | solution.py:19
  398.8 1.9 collective-permute-done.16
  400.6 5.2 %collective-permute-done.17 = bf16[8,128]{1,0:T(8,128)(2,1)S(1)} collective-permute-done((bf16[8,128]{1,0:T(8,128)(2,1)S(1)}, bf16[8,128]{1,0:T(8,128)(2,1)S(1)}, u32[]{:S(2)}, u32[]{:S(2)}) %collective-permute-start.17) | collective-permute-done | bytes 2080 | tf_op jit(solution)/shard_map/ppermute | solution.py:19
  (554 shorter events, 189.7 us)
Async XLA Ops:
  7.2 69.2 %all-gather.4.cloned.1.call-start = ((), (), s32[]{:S(2)}) async-start(), calls=%async_computation | async-start | bytes 1081344 | tf_op jit(solution)/shard_map/all_gather | solution.py:74
  7.9 133.7 %all-gather.6.cloned.1.call-start = ((), (), s32[]{:S(2)}) async-start(), calls=%async_computation.1 | async-start | bytes 1081344 | tf_op jit(solution)/shard_map/all_gather | solution.py:75
  8.7 0.7 copy-start
  187.6 22.5 %collective-permute-start = (f32[8,128,128]{2,1,0:T(8,128)S(1)}, f32[8,128,128]{2,1,0:T(8,128)S(1)}, u32[]{:S(2)}, u32[]{:S(2)}) collective-permute-start(f32[8,128,128]{2,1,0:T(8,128)S(1)} %get-tuple-element.198), channel_id=1, source_target_pairs={{224,0},{0,32},{32,64},{64,96},{96,128},{128,160},{160,192},{192,2... | collective-permute-start | bytes 1572872 | tf_op jit(solution)/shard_map/ppermute | solution.py:19
  190.4 19.5 %collective-permute-start.4 = (bf16[128,1024]{0,1:T(8,128)(2,1)S(1)}, bf16[128,1024]{0,1:T(8,128)(2,1)S(1)}, u32[]{:S(2)}, u32[]{:S(2)}) collective-permute-start(bf16[128,1024]{0,1:T(8,128)(2,1)S(1)} %copy.26), channel_id=1, source_target_pairs={{224,0},{0,32},{32,64},{64,96},{96,128},{128,160},{160,192},{192,2... | collective-permute-start | bytes 786440 | tf_op jit(solution)/shard_map/ppermute | solution.py:19
  191.2 18.8 %collective-permute-start.1 = (f32[8,128]{1,0:T(8,128)S(1)}, f32[8,128]{1,0:T(8,128)S(1)}, u32[]{:S(2)}, u32[]{:S(2)}) collective-permute-start(f32[8,128]{1,0:T(8,128)S(1)} %get-tuple-element.199), channel_id=1, source_target_pairs={{224,0},{0,32},{32,64},{64,96},{96,128},{128,160},{160,192},{192,2... | collective-permute-start | bytes 12296 | tf_op jit(solution)/shard_map/ppermute | solution.py:19
  194.0 16.1 %collective-permute-start.2 = (f32[8,128]{1,0:T(8,128)S(1)}, f32[8,128]{1,0:T(8,128)S(1)}, u32[]{:S(2)}, u32[]{:S(2)}) collective-permute-start(f32[8,128]{1,0:T(8,128)S(1)} %get-tuple-element.200), channel_id=1, source_target_pairs={{224,0},{0,32},{32,64},{64,96},{96,128},{128,160},{160,192},{192,2... | collective-permute-start | bytes 12296 | tf_op jit(solution)/shard_map/ppermute | solution.py:19
  195.7 14.4 %collective-permute-start.3 = (s32[128]{0:T(128)S(1)}, s32[128]{0:T(128)S(1)}, u32[]{:S(2)}, u32[]{:S(2)}) collective-permute-start(s32[128]{0:T(128)S(1)} %get-tuple-element.818), channel_id=1, source_target_pairs={{224,0},{0,32},{32,64},{64,96},{96,128},{128,160},{160,192},{192,2... | collective-permute-start | bytes 1544 | tf_op jit(solution)/shard_map/ppermute | solution.py:19
  256.1 21.5 %collective-permute-start.5 = (f32[8,128,128]{2,1,0:T(8,128)S(1)}, f32[8,128,128]{2,1,0:T(8,128)S(1)}, u32[]{:S(2)}, u32[]{:S(2)}) collective-permute-start(f32[8,128,128]{2,1,0:T(8,128)S(1)} %get-tuple-element.201), channel_id=1, source_target_pairs={{224,0},{0,32},{32,64},{64,96},{96,128},{128,160},{160,192},{192,2... | collective-permute-start | bytes 1572872 | tf_op jit(solution)/shard_map/ppermute | solution.py:19
  258.1 19.4 %collective-permute-start.9 = (bf16[128,1024]{0,1:T(8,128)(2,1)S(1)}, bf16[128,1024]{0,1:T(8,128)(2,1)S(1)}, u32[]{:S(2)}, u32[]{:S(2)}) collective-permute-start(bf16[128,1024]{0,1:T(8,128)(2,1)S(1)} %collective-permute-done.4), channel_id=1, source_target_pairs={{224,0},{0,32},{32,64},{64,96},{96,128},{128,160},{160,192},{192,2... | collective-permute-start | bytes 786440 | tf_op jit(solution)/shard_map/ppermute | solution.py:19
  261.0 16.7 %collective-permute-start.6 = (f32[8,128]{1,0:T(8,128)S(1)}, f32[8,128]{1,0:T(8,128)S(1)}, u32[]{:S(2)}, u32[]{:S(2)}) collective-permute-start(f32[8,128]{1,0:T(8,128)S(1)} %get-tuple-element.202), channel_id=1, source_target_pairs={{224,0},{0,32},{32,64},{64,96},{96,128},{128,160},{160,192},{192,2... | collective-permute-start | bytes 12296 | tf_op jit(solution)/shard_map/ppermute | solution.py:19
  261.6 16.1 %collective-permute-start.7 = (f32[8,128]{1,0:T(8,128)S(1)}, f32[8,128]{1,0:T(8,128)S(1)}, u32[]{:S(2)}, u32[]{:S(2)}) collective-permute-start(f32[8,128]{1,0:T(8,128)S(1)} %get-tuple-element.203), channel_id=1, source_target_pairs={{224,0},{0,32},{32,64},{64,96},{96,128},{128,160},{160,192},{192,2... | collective-permute-start | bytes 12296 | tf_op jit(solution)/shard_map/ppermute | solution.py:19
  264.2 13.5 %collective-permute-start.8 = (s32[128]{0:T(128)S(1)}, s32[128]{0:T(128)S(1)}, u32[]{:S(2)}, u32[]{:S(2)}) collective-permute-start(s32[128]{0:T(128)S(1)} %get-tuple-element.824), channel_id=1, source_target_pairs={{224,0},{0,32},{32,64},{64,96},{96,128},{128,160},{160,192},{192,2... | collective-permute-start | bytes 1544 | tf_op jit(solution)/shard_map/ppermute | solution.py:19
  323.7 20.7 %collective-permute-start.10 = (f32[8,128,128]{2,1,0:T(8,128)S(1)}, f32[8,128,128]{2,1,0:T(8,128)S(1)}, u32[]{:S(2)}, u32[]{:S(2)}) collective-permute-start(f32[8,128,128]{2,1,0:T(8,128)S(1)} %get-tuple-element.204), channel_id=1, source_target_pairs={{224,0},{0,32},{32,64},{64,96},{96,128},{128,160},{160,192},{192,2... | collective-permute-start | bytes 1572872 | tf_op jit(solution)/shard_map/ppermute | solution.py:19
  324.9 19.3 %collective-permute-start.14 = (bf16[128,1024]{0,1:T(8,128)(2,1)S(1)}, bf16[128,1024]{0,1:T(8,128)(2,1)S(1)}, u32[]{:S(2)}, u32[]{:S(2)}) collective-permute-start(bf16[128,1024]{0,1:T(8,128)(2,1)S(1)} %collective-permute-done.9), channel_id=1, source_target_pairs={{224,0},{0,32},{32,64},{64,96},{96,128},{128,160},{160,192},{192,2... | collective-permute-start | bytes 786440 | tf_op jit(solution)/shard_map/ppermute | solution.py:19
  329.9 14.5 %collective-permute-start.11 = (f32[8,128]{1,0:T(8,128)S(1)}, f32[8,128]{1,0:T(8,128)S(1)}, u32[]{:S(2)}, u32[]{:S(2)}) collective-permute-start(f32[8,128]{1,0:T(8,128)S(1)} %get-tuple-element.205), channel_id=1, source_target_pairs={{224,0},{0,32},{32,64},{64,96},{96,128},{128,160},{160,192},{192,2... | collective-permute-start | bytes 12296 | tf_op jit(solution)/shard_map/ppermute | solution.py:19
  330.0 14.4 %collective-permute-start.12 = (f32[8,128]{1,0:T(8,128)S(1)}, f32[8,128]{1,0:T(8,128)S(1)}, u32[]{:S(2)}, u32[]{:S(2)}) collective-permute-start(f32[8,128]{1,0:T(8,128)S(1)} %get-tuple-element.206), channel_id=1, source_target_pairs={{224,0},{0,32},{32,64},{64,96},{96,128},{128,160},{160,192},{192,2... | collective-permute-start | bytes 12296 | tf_op jit(solution)/shard_map/ppermute | solution.py:19
  332.0 12.4 %collective-permute-start.13 = (s32[128]{0:T(128)S(1)}, s32[128]{0:T(128)S(1)}, u32[]{:S(2)}, u32[]{:S(2)}) collective-permute-start(s32[128]{0:T(128)S(1)} %get-tuple-element.821), channel_id=1, source_target_pairs={{224,0},{0,32},{32,64},{64,96},{96,128},{128,160},{160,192},{192,2... | collective-permute-start | bytes 1544 | tf_op jit(solution)/shard_map/ppermute | solution.py:19
  390.6 15.9 %collective-permute-start.15 = (bf16[8,128,128]{2,1,0:T(8,128)(2,1)S(1)}, bf16[8,128,128]{2,1,0:T(8,128)(2,1)S(1)}, u32[]{:S(2)}, u32[]{:S(2)}) collective-permute-start(bf16[8,128,128]{2,1,0:T(8,128)(2,1)S(1)} %convert_element_type.39), channel_id=1, source_target_pairs={{96,0},{128,32},{160,64},{192,96},{224,128},{0,160},{32,192},{64,2... | collective-permute-start | bytes 786440 | tf_op jit(solution)/shard_map/ppermute | solution.py:19
  391.6 9.1 %collective-permute-start.16 = (bf16[8,128]{1,0:T(8,128)(2,1)S(1)}, bf16[8,128]{1,0:T(8,128)(2,1)S(1)}, u32[]{:S(2)}, u32[]{:S(2)}) collective-permute-start(bf16[8,128]{1,0:T(8,128)(2,1)S(1)} %convert_element_type.41), channel_id=1, source_target_pairs={{96,0},{128,32},{160,64},{192,96},{224,128},{0,160},{32,192},{64,2... | collective-permute-start | bytes 6152 | tf_op jit(solution)/shard_map/ppermute | solution.py:19
  398.7 7.2 %collective-permute-start.17 = (bf16[8,128]{1,0:T(8,128)(2,1)S(1)}, bf16[8,128]{1,0:T(8,128)(2,1)S(1)}, u32[]{:S(2)}, u32[]{:S(2)}) collective-permute-start(bf16[8,128]{1,0:T(8,128)(2,1)S(1)} %convert_element_type.46), channel_id=1, source_target_pairs={{96,0},{128,32},{160,64},{192,96},{224,128},{0,160},{32,192},{64,2... | collective-permute-start | bytes 6152 | tf_op jit(solution)/shard_map/ppermute | solution.py:19
Sparse Core Ops, SparseCore 0:
  9.9 66.5 all-gather.3
  78.3 63.2 all-gather.5
where the time goes:
time: 420 us; the launch traced here: 414 us
  matrix products  159 us (38%)
  waiting for transfers between devices  135 us (32%)
  starting transfers between devices  38.1 us (9%)
  blocking collectives  37 us (9%)
  other arithmetic  22.1 us (5%)
  between operations  14.3 us (3%)
  loops' own time  4.7 us (1%)
    dot_general x64, matrix products, tile_update(): jnp.einsum('htk,kd->htd', weights.astype(jnp.bfloat16), value_block, pref...  85.1 us
    dot_general x64, matrix products, tile_update(): jnp.einsum('thd,kd->htk', query_heads, key_block, preferred_element_type=...  73.7 us
    all_gather x1, waiting for transfers between devices, local(): lax.all_gather(values, 'col', axis=0, tiled=True)  65.2 us
    ppermute x18, waiting for transfers between devices, from_behind(): return lax.ppermute(block, axis, route)  41.4 us
    ppermute x18, starting transfers between devices, from_behind(): return lax.ppermute(block, axis, route)  38 us
    all_gather x1, blocking collectives, local(): lax.all_gather(positions, 'col', axis=0, tiled=True)  37 us
    all_gather x1, waiting for transfers between devices, local(): lax.all_gather(keys, 'col', axis=0, tiled=True)  27.4 us
    reduce_sum x64, other arithmetic, tile_update(): weight_total = weight_total * rescale + jnp.sum(weights, axis=-1)  12.4 us
  transfers between devices with their start and end apart: 20, of which 7 were waited for; matrix products, arithmetic and copies ran while one was open for 1% of the time, Pallas kernels for 0%

commit v1 on v0

v1 whole, which is shorter than its diff:
```python
import functools
import math

import jax
import jax.numpy as jnp
from jax import lax
from jax.experimental import pallas as pl
from jax.experimental.pallas import tpu as pltpu
from jax.sharding import PartitionSpec as P

HEADS = 8
HD = 128
TOK = 128
GROUPS = 8
NZ = 8
BLOCK = 2 * HD + 16
TO_LOG2 = math.log2(math.e) / math.sqrt(HD)
LN2 = math.log(2.0)
HIDDEN = -(2.0**100)
START = -1e30
ITEMS = 10

MESH = pl.DeviceIdType.MESH
F32 = jnp.float32
BF16 = jnp.bfloat16


def column_of(row_vector):
    return jnp.broadcast_to(row_vector, (TOK, TOK)).T


def kernel(
    q_ref, k_ref, v_ref, pos_ref, att_ref, log_ref,
    blocks, queries, places, place_out, place_in, eye, acc, top,
    part_out, part_in, lse_out, lse_in,
    col_send, col_recv, up_send, up_recv, down_send, down_recv, sib_send, sib_recv,
    q_send, q_recv, back_send, back_recv,
):
    row = lax.axis_index("row")
    col = lax.axis_index("col")
    lo = col // 16
    z = (col // 2) % NZ
    core = col % 2

    def place(lo_, z_, core_):
        return lo_ * 16 + z_ * 2 + core_

    partner = (row, place(1 - lo, z, core))
    sibling = (row, place(lo, z, 1 - core))
    above = (row, place(lo, (z + 1) % NZ, core))
    below = (row, place(lo, (z + NZ - 1) % NZ, core))
    before = (row + GROUPS - 1) % GROUPS
    after = (row + 1) % GROUPS
    before_at = [(before, place(l, z, core)) for l in range(2)]
    after_at = [(after, place(l, z, core)) for l in range(2)]
    queries_to = ((row + 2) % GROUPS, col)
    queries_from = ((row + GROUPS - 2) % GROUPS, col)

    barrier = pltpu.get_barrier_semaphore()
    partners = [partner, sibling, above, below, *before_at, *after_at, queries_to, queries_from]
    for device in partners:
        pl.semaphore_signal(barrier, inc=1, device_id=device, device_id_type=MESH)

    own = blocks.at[core, z, lo]
    own[0:HD, :] = k_ref[...].astype(F32).T.astype(BF16)
    own[HD : 2 * HD, :] = v_ref[...]
    pos = pos_ref[...]
    high, low = (pos // 256).astype(F32), (pos % 256).astype(F32)
    line = lax.broadcasted_iota(jnp.int32, (16, TOK), 0)
    coded = jnp.where(line == 0, high, jnp.where(line == 1, low, 0.0)).astype(BF16)
    own[2 * HD : BLOCK, :] = coded
    place_out[...] = coded
    queries[0] = q_ref[...]
    places[0] = column_of(high * 256.0 + low)
    eye[...] = (
        lax.broadcasted_iota(jnp.int32, (TOK, TOK), 0) == lax.broadcasted_iota(jnp.int32, (TOK, TOK), 1)
    ).astype(BF16)
    acc[...] = jnp.zeros_like(acc)
    top[...] = jnp.full_like(top, START)

    pl.semaphore_wait(barrier, len(partners))

    def remote(src, dst, send, recv, device):
        return pltpu.make_async_remote_copy(
            src_ref=src, dst_ref=dst, send_sem=send, recv_sem=recv, device_id=device, device_id_type=MESH
        )

    def column_copy(number, device, slot):
        return remote(own, blocks.at[core, z, slot], col_send.at[number], col_recv.at[slot], device)

    column = [
        column_copy(0, partner, lo),
        column_copy(1, before_at[0], 2 + lo),
        column_copy(2, before_at[1], 2 + lo),
    ]
    for copy in column:
        copy.start()
    send_places = remote(place_out, place_in, q_send.at[0], q_recv.at[0], queries_to)
    send_queries = remote(q_ref, queries.at[1], q_send.at[1], q_recv.at[1], queries_to)
    send_places.start()
    send_queries.start()

    def z_at(distance):
        return (z + NZ + distance) % NZ

    def ring(step, up):
        bundle = z_at(-step if up else step)
        part = blocks.at[core, bundle]
        if step == 3:
            part = part.at[pl.ds(0, 2)] if up else part.at[pl.ds(2, 2)]
        if up:
            return remote(part, part, up_send.at[step], up_recv.at[step], above)
        return remote(part, part, down_send.at[step], down_recv.at[step], below)

    def arrived(step, up):
        bundle = z_at(-(step + 1) if up else step + 1)
        part = blocks.at[core, bundle]
        if step == 3:
            part = part.at[pl.ds(0, 2)] if up else part.at[pl.ds(2, 2)]
        if up:
            remote(part, part, up_send.at[step], up_recv.at[step], above).wait_recv()
        else:
            remote(part, part, down_send.at[step], down_recv.at[step], below).wait_recv()

    def across(number, distance):
        part = blocks.at[core, z_at(distance)]
        return remote(part, part, sib_send.at[number], sib_recv.at[number], sibling)

    def from_sibling(number, distance):
        part = blocks.at[1 - core, z_at(distance)]
        remote(part, part, sib_send.at[number], sib_recv.at[number], sibling).wait_recv()

    for slot, device in ((1 - lo, partner), (2, after_at[0]), (3, after_at[1])):
        remote(own, blocks.at[core, z, slot], col_send.at[0], col_recv.at[slot], device).wait_recv()
    ring(0, True).start()
    ring(0, False).start()
    across(0, 0).start()
    from_sibling(0, 0)

    def attend(which, spots):
        parts = [blocks.at[c, spot, j] for spot in spots for c in range(2) for j in range(4)]
        count = len(parts)
        keys = jnp.concatenate([part[0:HD, :] for part in parts], axis=1)
        values = jnp.concatenate([part[HD : 2 * HD, :] for part in parts], axis=0)
        values = jnp.concatenate([values, jnp.ones((count * TOK, HD), BF16)], axis=1)
        own_place = places[which]
        bias = []
        for part in parts:
            key_place = part[2 * HD : 2 * HD + 1, :].astype(F32) * 256.0 + part[2 * HD + 1 : 2 * HD + 2, :].astype(F32)
            bias.append(jnp.where(key_place <= own_place, 0.0, HIDDEN).astype(BF16))
        keys = jnp.concatenate([keys, jnp.concatenate(bias, axis=1)], axis=0)
        for head in range(HEADS):
            rows = pl.ds(head * TOK, TOK)
            left = jnp.concatenate([queries[which, :, head * HD : (head + 1) * HD], eye[...]], axis=1)
            scores = jnp.dot(left, keys, preferred_element_type=F32)
            most = scores[:, 0:TOK]
            for i in range(1, count):
                most = jnp.maximum(most, scores[:, i * TOK : (i + 1) * TOK])
            old = top[which, rows, :]
            new = jnp.maximum(old, jnp.max(most, axis=1, keepdims=True) * TO_LOG2)
            fade = jnp.exp2(old - new)
            top[which, rows, :] = new
            weights = jnp.concatenate(
                [jnp.exp2(scores[:, i * TOK : (i + 1) * TOK] * TO_LOG2 - new).astype(BF16) for i in range(count)],
                axis=1,
            )
            acc[which, rows, :] = acc[which, rows, :] * jnp.concatenate([fade, fade], axis=1) + jnp.dot(
                weights, values, preferred_element_type=F32
            )

    def item(i, carry):
        other = (i == 1) | (i == 2) | (i == 4) | (i == 6) | (i == 7)
        which = jnp.where(other, 1, 0)
        distance = jnp.where(i < 7, i // 2, jnp.where(i == 8, 3, 4))

        @pl.when(i == 1)
        def _():
            send_places.wait_recv()
            send_queries.wait_recv()
            got = place_in[...].astype(F32)
            places[1] = column_of(got[0:1, :] * 256.0 + got[1:2, :])

        for step in range(3):

            @pl.when(i == 2 * step + 2)
            def _(step=step):
                arrived(step, True)
                ring(step + 1, True).start()
                across(2 * step + 1, -(step + 1)).start()
                arrived(step, False)
                ring(step + 1, False).start()
                across(2 * step + 2, step + 1).start()
                from_sibling(2 * step + 1, -(step + 1))
                from_sibling(2 * step + 2, step + 1)

        @pl.when(i == 7)
        def _():
            arrived(3, True)
            arrived(3, False)
            across(7, 4).start()
            from_sibling(7, 4)

        single = (distance == 0) | (distance == 4)

        @pl.when(single)
        def _():
            attend(which, [(z + distance) % NZ])

        @pl.when(jnp.logical_not(single))
        def _():
            attend(which, [(z + NZ - distance) % NZ, (z + distance) % NZ])

        @pl.when(i == 7)
        def _():
            for head in range(HEADS):
                rows = pl.ds(head * TOK, TOK)
                total = acc[1, rows, HD:]
                part_out[rows, :] = (acc[1, rows, 0:HD] / total).astype(BF16)
                lse = top[1, rows, :] + jnp.log2(total)
                lse_out[head : head + 1, :] = jnp.sum(jnp.where(eye[...] != 0, lse, 0.0), axis=0, keepdims=True)
            remote(part_out, part_in, back_send.at[0], back_recv.at[0], queries_from).start()
            remote(lse_out, lse_in, back_send.at[1], back_recv.at[1], queries_from).start()

        return carry

    lax.fori_loop(0, ITEMS, item, 0)

    part_back = remote(part_out, part_in, back_send.at[0], back_recv.at[0], queries_from)
    lse_back = remote(lse_out, lse_in, back_send.at[1], back_recv.at[1], queries_from)
    lse_back.wait_recv()
    part_back.wait_recv()
    for head in range(HEADS):
        rows = pl.ds(head * TOK, TOK)
        total = acc[0, rows, HD:]
        mine = top[0, rows, :] + jnp.log2(total)
        theirs = column_of(lse_in[head : head + 1, :])
        larger = jnp.maximum(mine, theirs)
        share, other_share = jnp.exp2(mine - larger), jnp.exp2(theirs - larger)
        both = share + other_share
        result = acc[0, rows, 0:HD] * (share / (total * both)) + part_in[rows, :].astype(F32) * (other_share / both)
        att_ref[:, head * HD : (head + 1) * HD] = result.astype(BF16)
        lse = (larger + jnp.log2(both)) * LN2
        log_ref[head : head + 1, :] = jnp.sum(jnp.where(eye[...] != 0, lse, 0.0), axis=0, keepdims=True)

    for copy in column:
        copy.wait_send()
    send_places.wait_send()
    send_queries.wait_send()
    for step in range(4):
        ring(step, True).wait_send()
        ring(step, False).wait_send()
    across(0, 0).wait_send()
    for step in range(3):
        across(2 * step + 1, -(step + 1)).wait_send()
        across(2 * step + 2, step + 1).wait_send()
    across(7, 4).wait_send()
    part_back.wait_send()
    lse_back.wait_send()


def local(queries, keys, values, positions):
    vmem = pl.BlockSpec(memory_space=pltpu.VMEM)
    dma = pltpu.SemaphoreType.DMA
    return pl.pallas_call(
        kernel,
        out_shape=(
            jax.ShapeDtypeStruct((TOK, HEADS * HD), BF16),
            jax.ShapeDtypeStruct((HEADS, TOK), F32),
        ),
        in_specs=[vmem] * 4,
        out_specs=(vmem, vmem),
        scratch_shapes=[
            pltpu.VMEM((2, NZ, 4, BLOCK, HD), BF16),
            pltpu.VMEM((2, TOK, HEADS * HD), BF16),
            pltpu.VMEM((2, TOK, TOK), F32),
            pltpu.VMEM((16, TOK), BF16),
            pltpu.VMEM((16, TOK), BF16),
            pltpu.VMEM((TOK, TOK), BF16),
            pltpu.VMEM((2, HEADS * TOK, 2 * HD), F32),
            pltpu.VMEM((2, HEADS * TOK, TOK), F32),
            pltpu.VMEM((HEADS * TOK, HD), BF16),
            pltpu.VMEM((HEADS * TOK, HD), BF16),
            pltpu.VMEM((HEADS, TOK), F32),
            pltpu.VMEM((HEADS, TOK), F32),
            dma((3,)), dma((4,)),
            dma((4,)), dma((4,)), dma((4,)), dma((4,)),
            dma((8,)), dma((8,)),
            dma((2,)), dma((2,)), dma((2,)), dma((2,)),
        ],
        compiler_params=pltpu.CompilerParams(
            collective_id=0, has_side_effects=True, vmem_limit_bytes=48 * 2**20
        ),
    )(queries, keys, values, positions.reshape(1, TOK))


def solution(mesh):
    placed = (
        P(("row", "col"), None),
        P(("row", "col"), None),
        P(("row", "col"), None),
        P(("row", "col")),
    )
    return jax.shard_map(
        local,
        mesh=mesh,
        in_specs=placed,
        out_specs=(P(("row", "col"), None), P(None, ("row", "col"))),
        check_vma=False,
    )
```

time: 420 us -> 59.4 us (0.14)
  the two profiles are of different devices: /device:TPU:6 before, /device:TPU:1 now
where the time goes in v1:
time: 59.4 us; the launch traced here: 58.2 us
  Pallas kernels  53.1 us (89%)
  local copies, waits for them, and re-layouts  4.41 us (7%)
  between operations  0.65 us (1%)
    pallas_call x1, Pallas kernels, local(): pl.pallas_call(kernel, out_shape=(jax.ShapeDtypeStruct((TOK, HEADS * HD),...  53.1 us
    unnamed x10, local copies, waits for them, and re-layouts  4.41 us

profile of v1, /device:TPU:1, one launch (start us, length us, event | category | flops | bytes accessed | tf_op | source)
XLA Modules:
  0.0 58.2 jit_solution(268046120134250293)
XLA Ops:
  0.6 0.0 copy-start.3
  0.6 0.6 %copy-done.3 = s32[128]{0:T(128)S(1)} copy-done((s32[128]{0:T(128)S(1)}, s32[128]{0:T(128)}, u32[]{:S(2)}) %copy-start.3) | copy-done | bytes 536
  1.3 0.0 copy-start
  1.3 0.9 %copy-done = bf16[128,1024]{1,0:T(8,128)(2,1)S(1)} copy-done((bf16[128,1024]{1,0:T(8,128)(2,1)S(1)}, bf16[128,1024]{1,0:T(8,128)(2,1)}, u32[]{:S(2)}) %copy-start) | copy-done | bytes 262168
  2.2 0.0 copy-start.1
  2.2 0.8 %copy-done.1 = bf16[128,128]{1,0:T(8,128)(2,1)S(1)} copy-done((bf16[128,128]{1,0:T(8,128)(2,1)S(1)}, bf16[128,128]{1,0:T(8,128)(2,1)}, u32[]{:S(2)}) %copy-start.1) | copy-done | bytes 32792
  3.0 0.0 copy-start.2
  3.0 0.8 %copy-done.2 = bf16[128,128]{1,0:T(8,128)(2,1)S(1)} copy-done((bf16[128,128]{1,0:T(8,128)(2,1)S(1)}, bf16[128,128]{1,0:T(8,128)(2,1)}, u32[]{:S(2)}) %copy-start.2) | copy-done | bytes 32792
  3.8 53.1 %shard_map.59 = (bf16[128,1024]{1,0:T(8,128)(2,1)S(1)}, f32[8,128]{1,0:T(8,128)S(1)}) custom-call(bf16[128,1024]{1,0:T(8,128)(2,1)S(1)} %copy-done, bf16[128,128]{1,0:T(8,128)(2,1)S(1)} %copy-done.1, bf16[128,128]{1,0:T(8,128)(2,1)S(1)} %copy-done.2, s32[1,128]{1,0:T(1,128)S(1)} %bitcast.1), custom_call_target="tpu_custom_call" | custom-call | tf_op jit(solution)/shard_map/pallas_call | solution.py:264
  56.9 0.7 %copy.8 = bf16[128,1024]{1,0:T(8,128)(2,1)} copy(bf16[128,1024]{1,0:T(8,128)(2,1)S(1)} %get-tuple-element.4) | data formatting | bytes 524288
  57.6 0.6 %copy.9 = f32[8,128]{1,0:T(8,128)} copy(f32[8,128]{1,0:T(8,128)S(1)} %get-tuple-element.5) | data formatting | bytes 8192
Async XLA Ops:
  0.6 0.7 %copy-start.3 = (s32[128]{0:T(128)S(1)}, s32[128]{0:T(128)}, u32[]{:S(2)}) copy-start(s32[128]{0:T(128)} %param.7) | copy-start | bytes 1540
  1.3 0.9 %copy-start = (bf16[128,1024]{1,0:T(8,128)(2,1)S(1)}, bf16[128,1024]{1,0:T(8,128)(2,1)}, u32[]{:S(2)}) copy-start(bf16[128,1024]{1,0:T(8,128)(2,1)} %q_ref.1) | copy-start | bytes 786436
  2.2 0.8 %copy-start.1 = (bf16[128,128]{1,0:T(8,128)(2,1)S(1)}, bf16[128,128]{1,0:T(8,128)(2,1)}, u32[]{:S(2)}) copy-start(bf16[128,128]{1,0:T(8,128)(2,1)} %k_ref.1) | copy-start | bytes 98308
  3.0 0.8 %copy-start.2 = (bf16[128,128]{1,0:T(8,128)(2,1)S(1)}, bf16[128,128]{1,0:T(8,128)(2,1)}, u32[]{:S(2)}) copy-start(bf16[128,128]{1,0:T(8,128)(2,1)} %v_ref.1) | copy-start | bytes 98308

commit v2 on v1

v2 whole, which is shorter than its diff:
```python
import functools
import math

import jax
import jax.numpy as jnp
from jax import lax
from jax.experimental import pallas as pl
from jax.experimental.pallas import tpu as pltpu
from jax.sharding import PartitionSpec as P

HEADS = 8
HD = 128
TOK = 128
GROUPS = 8
NZ = 8
BLOCK = 2 * HD + 16
TO_LOG2 = math.log2(math.e) / math.sqrt(HD)
LN2 = math.log(2.0)
HIDDEN = -(2.0**100)
START = -1e30
ITEMS = 10
BACK_ROWS = 256
OFFSETS = (0, 1, -1, 2, -2, 3, -3, 4)
HALF = 144
SMALL = (
    ((0, 0), (1, 0), (2, 0), (0, 1)),
    ((2, 7), (3, 7), (3, 5), (3, 6)),
)
LARGE = (
    ((0, 2), (3, 0), (1, 1), (1, 2), (2, 1), (2, 2), (0, 3), (0, 4)),
    ((3, 1), (3, 2), (1, 3), (1, 4), (2, 3), (2, 4), (0, 5), (0, 6)),
    ((3, 3), (3, 4), (1, 5), (1, 6), (2, 5), (2, 6), (0, 7), (1, 7)),
)

MESH = pl.DeviceIdType.MESH
F32 = jnp.float32
BF16 = jnp.bfloat16


def column_of(row_vector):
    return jnp.broadcast_to(row_vector, (TOK, TOK)).T


def kernel(
    q_hbm, k_hbm, v_hbm, pos_hbm, att_ref, log_ref,
    blocks, queries, key_in, pos_in, places, place_out, place_in, eye, acc, top,
    part_out, part_in, lse_out, lse_in,
    load, z_send, half_recv, column_send, line_recv, partner_send, near_send, far_send, sib_send, sib_recv,
    q_send, q_recv, back_send, back_recv, lse_send, lse_recv,
):
    row = lax.axis_index("row")
    col = lax.axis_index("col")
    lo = col // 16
    z = (col // 2) % NZ
    core = col % 2

    def spot(distance):
        return (z + NZ + distance) % NZ

    def at(row_, lo_, z_, core_):
        return ((row_ + GROUPS) % GROUPS, lo_ * 16 + z_ * 2 + core_)

    partner = at(row, 1 - lo, z, core)
    sibling = at(row, lo, z, 1 - core)
    near_before = at(row - 2, lo, z, core)
    near_after = at(row + 2, lo, z, core)
    queries_to = at(row + 1, 1 - lo, z, core)
    queries_from = at(row - 1, 1 - lo, z, core)
    along_z = {d: at(row, lo, spot(d), core) for d in (1, -1, 2, -2)}

    own = blocks.at[core, z, 0]
    loads = [
        pltpu.make_async_copy(k_hbm, key_in, load.at[0]),
        pltpu.make_async_copy(v_hbm, own.at[pl.ds(HD, HD)], load.at[1]),
        pltpu.make_async_copy(pos_hbm, pos_in, load.at[2]),
        pltpu.make_async_copy(q_hbm, queries.at[0], load.at[3]),
    ]
    for copy in loads:
        copy.start()

    barrier = pltpu.get_barrier_semaphore()
    partners = [partner, sibling, near_before, near_after, queries_to, queries_from, *along_z.values()]
    for device in partners:
        pl.semaphore_signal(barrier, inc=1, device_id=device, device_id_type=MESH)

    eye[...] = (
        lax.broadcasted_iota(jnp.int32, (TOK, TOK), 0) == lax.broadcasted_iota(jnp.int32, (TOK, TOK), 1)
    ).astype(BF16)
    acc[...] = jnp.zeros_like(acc)
    top[...] = jnp.full_like(top, START)
    for copy in loads:
        copy.wait()

    own[0:HD, :] = key_in[...].astype(F32).T.astype(BF16)
    pos = pos_in[...]
    high, low = (pos // 256).astype(F32), (pos % 256).astype(F32)
    line = lax.broadcasted_iota(jnp.int32, (16, TOK), 0)
    coded = jnp.where(line == 0, high, jnp.where(line == 1, low, 0.0)).astype(BF16)
    own[2 * HD : BLOCK, :] = coded
    place_out[...] = coded
    places[0] = column_of(high * 256.0 + low)

    pl.semaphore_wait(barrier, len(partners))

    def remote(src, dst, send, recv, device):
        return pltpu.make_async_remote_copy(
            src_ref=src, dst_ref=dst, send_sem=send, recv_sem=recv, device_id=device, device_id_type=MESH
        )

    def block(line_, e, core_=None):
        return blocks.at[core if core_ is None else core_, spot(OFFSETS[e]), line_]

    def z_copy(n):
        d = (1, -1, 2, -2, 1, -1, 2, -2)[n]
        if n < 4:
            return remote(own, own, z_send.at[n], line_recv.at[0, OFFSETS.index(-d)], along_z[d])
        came = -2 if d > 0 else 2
        ref = block(0, OFFSETS.index(came))
        if n < 6:
            return remote(ref, ref, z_send.at[n], line_recv.at[0, OFFSETS.index(came - d)], along_z[d])
        ref = ref.at[pl.ds(0, HALF)] if d > 0 else ref.at[pl.ds(HALF, BLOCK - HALF)]
        return remote(ref, ref, z_send.at[n], half_recv.at[n - 6], along_z[d])

    def column_copy(n):
        d = (1, -1)[n % 2]
        ref = blocks.at[core, z, pl.ds(1, 2) if n < 2 else pl.ds(3, 1)]
        return remote(ref, ref, column_send.at[n], line_recv.at[1 if n < 2 else 3, OFFSETS.index(-d)], along_z[d])

    def partner_copy(e):
        return remote(block(0, e), block(2, e), partner_send.at[e], line_recv.at[2, e], partner)

    def near_copy(e):
        return remote(block(0, e), block(1, e), near_send.at[e], line_recv.at[1, e], near_before)

    far_to = tuple(jnp.where(core == 0, p, n) for p, n in zip(partner, near_before))

    def far_copy(e):
        return remote(block(1 + core, e), block(3, e), far_send.at[e], line_recv.at[3, e], far_to)

    def sib_copy(part, e, core_=None):
        first, count = ((0, 1), (1, 2), (3, 1))[part]
        ref = blocks.at[core if core_ is None else core_, spot(OFFSETS[e]), pl.ds(first, count)]
        return remote(ref, ref, sib_send.at[part, e], sib_recv.at[part, e], sibling)

    def arrived(line_, e):
        if line_ == 0 and e == 7:
            for n in range(2):
                z_copy(6 + n).wait_recv()
            return
        ref = block(line_, e)
        if line_ == 1 and e in (1, 2):
            ref = blocks.at[core, spot(OFFSETS[e]), pl.ds(1, 2)]
        remote(ref, ref, z_send.at[0], line_recv.at[line_, e], sibling).wait_recv()

    def pass_on(e):
        if e > 0:
            arrived(0, e)
        if e == 4:
            z_copy(4).start()
            z_copy(6).start()
        if e == 3:
            z_copy(5).start()
            z_copy(7).start()
        if e not in (1, 2):
            partner_copy(e).start()
            near_copy(e).start()
        sib_copy(0, e).start()

    def pass_far(e):
        arrived(1, e)
        if e not in (1, 2):
            arrived(2, e)
            far_copy(e).start()
        if e == 0:
            column_copy(0).start()
            column_copy(1).start()
        sib_copy(1, e).start()

    def pass_last(e):
        arrived(3, e)
        if e == 0:
            column_copy(2).start()
            column_copy(3).start()
        sib_copy(2, e).start()

    def from_sibling(part, e):
        sib_copy(part, e, 1 - core).wait_recv()

    def need(messages):
        for part, e in messages:
            from_sibling(part, e)

    for n in (0, 1):
        z_copy(n).start()
    pass_on(0)
    send_places = remote(place_out, place_in, q_send.at[0], q_recv.at[0], queries_to)
    send_queries = remote(queries.at[0], queries.at[1], q_send.at[1], q_recv.at[1], queries_to)
    for n in (2, 3):
        z_copy(n).start()
    send_places.start()
    send_queries.start()
    pass_far(0)
    pass_on(1)
    pass_on(2)
    need(((0, 0), (0, 1), (1, 0)))

    def attend(which, spots):
        parts = [blocks.at[c, zz, j] for zz, j in spots for c in range(2)]
        count = len(parts)
        keys = jnp.concatenate([part[0:HD, :] for part in parts], axis=1)
        values = jnp.concatenate([part[HD : 2 * HD, :] for part in parts], axis=0)
        values = jnp.concatenate([values, jnp.ones((count * TOK, HD), BF16)], axis=1)
        own_place = places[which]
        bias = []
        for part in parts:
            key_place = part[2 * HD : 2 * HD + 1, :].astype(F32) * 256.0 + part[2 * HD + 1 : 2 * HD + 2, :].astype(F32)
            bias.append(jnp.where(key_place <= own_place, 0.0, HIDDEN).astype(BF16))
        keys = jnp.concatenate([keys, jnp.concatenate(bias, axis=1)], axis=0)
        for head in range(HEADS):
            rows = pl.ds(head * TOK, TOK)
            left = jnp.concatenate([queries[which, :, head * HD : (head + 1) * HD], eye[...]], axis=1)
            scores = jnp.dot(left, keys, preferred_element_type=F32)
            most = scores[:, 0:TOK]
            for i in range(1, count):
                most = jnp.maximum(most, scores[:, i * TOK : (i + 1) * TOK])
            old = top[which, rows, :]
            new = jnp.maximum(old, jnp.max(most, axis=1, keepdims=True) * TO_LOG2)
            fade = jnp.exp2(old - new)
            top[which, rows, :] = new
            weights = jnp.concatenate(
                [jnp.exp2(scores[:, i * TOK : (i + 1) * TOK] * TO_LOG2 - new).astype(BF16) for i in range(count)],
                axis=1,
            )
            acc[which, rows, :] = acc[which, rows, :] * jnp.concatenate([fade, fade], axis=1) + jnp.dot(
                weights, values, preferred_element_type=F32
            )

    def back_copy(n):
        rows = pl.ds(n * BACK_ROWS, BACK_ROWS)
        return remote(part_out.at[rows], part_in.at[rows], back_send.at[n], back_recv.at[n], queries_from)

    lse_copy = remote(lse_out, lse_in, lse_send.at[0], lse_recv.at[0], queries_from)

    def early(i):
        if i == 1:
            pass_last(0)
            pass_on(3)
            pass_on(4)
            send_places.wait_recv()
            send_queries.wait_recv()
            got = place_in[...].astype(F32)
            places[1] = column_of(got[0:1, :] * 256.0 + got[1:2, :])
        elif i == 2:
            pass_far(1)
            pass_far(2)
            need(((0, 2), (2, 0), (1, 1), (1, 2), (0, 3), (0, 4)))
        elif i == 3:
            pass_on(5)
            pass_on(6)
            pass_last(1)
            pass_last(2)
            pass_far(3)
            pass_far(4)
        elif i == 4:
            pass_on(7)
            need(((2, 1), (2, 2), (1, 3), (1, 4), (0, 5), (0, 6)))
        elif i == 5:
            pass_far(5)
            pass_far(6)
            pass_far(7)
            pass_last(3)
            pass_last(4)
        elif i == 6:
            need(((2, 3), (2, 4), (1, 5), (1, 6), (0, 7), (1, 7)))
            pass_last(5)
            pass_last(6)
            pass_last(7)
        elif i == 7:
            need(((2, 7), (2, 5), (2, 6)))

    def give_back():
        for head in range(HEADS):
            rows = pl.ds(head * TOK, TOK)
            total = acc[1, rows, HD:]
            part_out[rows, :] = (acc[1, rows, 0:HD] / total).astype(BF16)
            if (head + 1) * TOK % BACK_ROWS == 0:
                back_copy((head + 1) * TOK // BACK_ROWS - 1).start()
            lse = top[1, rows, :] + jnp.log2(total)
            lse_out[head : head + 1, :] = jnp.sum(jnp.where(eye[...] != 0, lse, 0.0), axis=0, keepdims=True)
        lse_copy.start()

    def choose(index, tiles):
        found = []
        for choices in zip(*tiles):
            line_, distance = choices[-1][0], OFFSETS[choices[-1][1]]
            for n in range(len(tiles) - 1):
                line_ = jnp.where(index == n, choices[n][0], line_)
                distance = jnp.where(index == n, OFFSETS[choices[n][1]], distance)
            found.append((spot(distance), line_))
        return found

    def item(i, carry):
        other = (i == 1) | (i == 2) | (i == 4) | (i == 6) | (i == 7)
        which = jnp.where(other, 1, 0)
        for n in range(1, 8):

            @pl.when(i == n)
            def _(n=n):
                early(n)

        small = (i < 2) | (i == 7) | (i == 9)

        @pl.when(small)
        def _():
            attend(which, choose(jnp.where(i < 2, 0, 1), SMALL))

        @pl.when(jnp.logical_not(small))
        def _():
            attend(which, choose(jnp.where(i == 8, 2, i // 2 - 1), LARGE))

        @pl.when(i == 7)
        def _():
            give_back()

        return carry

    lax.fori_loop(0, ITEMS, item, 0)

    lse_copy.wait_recv()
    for head in range(HEADS):
        rows = pl.ds(head * TOK, TOK)
        if head * TOK % BACK_ROWS == 0:
            back_copy(head * TOK // BACK_ROWS).wait_recv()
        total = acc[0, rows, HD:]
        mine = top[0, rows, :] + jnp.log2(total)
        theirs = column_of(lse_in[head : head + 1, :])
        larger = jnp.maximum(mine, theirs)
        share, other_share = jnp.exp2(mine - larger), jnp.exp2(theirs - larger)
        both = share + other_share
        result = acc[0, rows, 0:HD] * (share / (total * both)) + part_in[rows, :].astype(F32) * (other_share / both)
        att_ref[:, head * HD : (head + 1) * HD] = result.astype(BF16)
        lse = (larger + jnp.log2(both)) * LN2
        log_ref[head : head + 1, :] = jnp.sum(jnp.where(eye[...] != 0, lse, 0.0), axis=0, keepdims=True)

    for n in range(8):
        z_copy(n).wait_send()
    for n in range(4):
        column_copy(n).wait_send()
    for e in range(NZ):
        if e not in (1, 2):
            partner_copy(e).wait_send()
            near_copy(e).wait_send()
            far_copy(e).wait_send()
        for part in range(3):
            sib_copy(part, e).wait_send()
    send_places.wait_send()
    send_queries.wait_send()
    for n in range(HEADS * TOK // BACK_ROWS):
        back_copy(n).wait_send()
    lse_copy.wait_send()


def local(queries, keys, values, positions):
    vmem = pl.BlockSpec(memory_space=pltpu.VMEM)
    hbm = pl.BlockSpec(memory_space=pltpu.HBM)
    dma = pltpu.SemaphoreType.DMA
    backs = HEADS * TOK // BACK_ROWS
    return pl.pallas_call(
        kernel,
        out_shape=(
            jax.ShapeDtypeStruct((TOK, HEADS * HD), BF16),
            jax.ShapeDtypeStruct((HEADS, TOK), F32),
        ),
        in_specs=[hbm] * 4,
        out_specs=(vmem, vmem),
        scratch_shapes=[
            pltpu.VMEM((2, NZ, 4, BLOCK, HD), BF16),
            pltpu.VMEM((2, TOK, HEADS * HD), BF16),
            pltpu.VMEM((TOK, HD), BF16),
            pltpu.VMEM((1, TOK), jnp.int32),
            pltpu.VMEM((2, TOK, TOK), F32),
            pltpu.VMEM((16, TOK), BF16),
            pltpu.VMEM((16, TOK), BF16),
            pltpu.VMEM((TOK, TOK), BF16),
            pltpu.VMEM((2, HEADS * TOK, 2 * HD), F32),
            pltpu.VMEM((2, HEADS * TOK, TOK), F32),
            pltpu.VMEM((HEADS * TOK, HD), BF16),
            pltpu.VMEM((HEADS * TOK, HD), BF16),
            pltpu.VMEM((HEADS, TOK), F32),
            pltpu.VMEM((HEADS, TOK), F32),
            dma((4,)), dma((8,)), dma((2,)), dma((4,)), dma((4, NZ)), dma((NZ,)), dma((NZ,)), dma((NZ,)), dma((3, NZ)), dma((3, NZ)),
            dma((2,)), dma((2,)), dma((backs,)), dma((backs,)), dma((1,)), dma((1,)),
        ],
        compiler_params=pltpu.CompilerParams(
            collective_id=0, has_side_effects=True, vmem_limit_bytes=63 * 2**20
        ),
    )(queries, keys, values, positions.reshape(1, TOK))


def solution(mesh):
    placed = (
        P(("row", "col"), None),
        P(("row", "col"), None),
        P(("row", "col"), None),
        P(("row", "col")),
    )
    return jax.shard_map(
        local,
        mesh=mesh,
        in_specs=placed,
        out_specs=(P(("row", "col"), None), P(None, ("row", "col"))),
        check_vma=False,
    )
```

time: 59.4 us -> 54.5 us (0.918); the launches traced: 58.2 us -> 54.4 us
  local copies, waits for them, and re-layouts: 4.41 us -> 2.27 us
  Pallas kernels: 53.1 us -> 51.5 us
    unnamed x10 -> x4, local copies, waits for them, and re-layouts: 4.41 us -> 2.27 us
    pallas_call x1, Pallas kernels: 53.1 us -> 51.5 us  [local(): pl.pallas_call(kernel, out_shape=(jax.ShapeDtypeStruct((TOK, HEADS * HD),...]
where the time goes in v2:
time: 54.5 us; the launch traced here: 54.4 us
  Pallas kernels  51.5 us (94%)
  local copies, waits for them, and re-layouts  2.27 us (4%)
  between operations  0.65 us (1%)
    pallas_call x1, Pallas kernels, local(): pl.pallas_call(kernel, out_shape=(jax.ShapeDtypeStruct((TOK, HEADS * HD),...  51.5 us
    unnamed x4, local copies, waits for them, and re-layouts  2.27 us

profile of v2, /device:TPU:1, one launch (start us, length us, event | category | flops | bytes accessed | tf_op | source)
XLA Modules:
  0.0 54.4 jit_solution(7473282044042914409)
XLA Ops:
  0.6 51.5 %shard_map.59 = (bf16[128,1024]{1,0:T(8,128)(2,1)}, f32[8,128]{1,0:T(8,128)}) custom-call(bf16[128,1024]{1,0:T(8,128)(2,1)} %q_hbm.1, bf16[128,128]{1,0:T(8,128)(2,1)} %k_hbm.1, bf16[128,128]{1,0:T(8,128)(2,1)} %v_hbm.1, s32[1,128]{1,0:T(1,128)} %bitcast.1), custom_call_target="tpu_custom_call" | custom-call | tf_op jit(solution)/shard_map/pallas_call | solution.py:368
  52.1 0.0 copy-start
  52.1 1.7 %copy.8 = bf16[128,1024]{1,0:T(8,128)(2,1)} copy(bf16[128,1024]{1,0:T(8,128)(2,1)} %get-tuple-element.4) | data formatting | bytes 524288
  53.8 0.0 copy-done
  53.8 0.6 %copy.9 = f32[8,128]{1,0:T(8,128)} copy(f32[8,128]{1,0:T(8,128)S(1)} %copy-done) | data formatting | bytes 8192
Async XLA Ops:
  52.1 1.7 %copy-start = (f32[8,128]{1,0:T(8,128)S(1)}, f32[8,128]{1,0:T(8,128)}, u32[]{:S(2)}) copy-start(f32[8,128]{1,0:T(8,128)} %get-tuple-element.5) | copy-start | bytes 12292

commit v3 on v2

--- a/solution.py
+++ b/solution.py
@@ -18,19 +18,29 @@
 LN2 = math.log(2.0)
 HIDDEN = -(2.0**100)
 START = -1e30
-ITEMS = 10
+ITEMS = 12
 BACK_ROWS = 256
 OFFSETS = (0, 1, -1, 2, -2, 3, -3, 4)
 HALF = 144
-SMALL = (
+DIRECT = (7,)
+STAGES = (
     ((0, 0), (1, 0), (2, 0), (0, 1)),
-    ((2, 7), (3, 7), (3, 5), (3, 6)),
-)
-LARGE = (
     ((0, 2), (3, 0), (1, 1), (1, 2), (2, 1), (2, 2), (0, 3), (0, 4)),
     ((3, 1), (3, 2), (1, 3), (1, 4), (2, 3), (2, 4), (0, 5), (0, 6)),
     ((3, 3), (3, 4), (1, 5), (1, 6), (2, 5), (2, 6), (0, 7), (1, 7)),
+    ((2, 7), (3, 7), (3, 5), (3, 6)),
 )
+
+
+def tile(own_stage, other_stage):
+    own = STAGES[own_stage] if own_stage is not None else ()
+    other = STAGES[other_stage] if other_stage is not None else ()
+    return tuple((0, *b) for b in own) + tuple((1, *b) for b in other)
+
+
+SMALL = (tile(0, None), tile(None, 4))
+MIDDLE = (tile(1, 0), tile(4, 3))
+LARGE = (tile(2, 1), tile(3, 2))
 
 MESH = pl.DeviceIdType.MESH
 F32 = jnp.float32
@@ -64,6 +74,8 @@
     sibling = at(row, lo, z, 1 - core)
     near_before = at(row - 2, lo, z, core)
     near_after = at(row + 2, lo, z, core)
+    far_before = at(row - 2, 1 - lo, z, core)
+    far_after = at(row + 2, 1 - lo, z, core)
     queries_to = at(row + 1, 1 - lo, z, core)
     queries_from = at(row - 1, 1 - lo, z, core)
     along_z = {d: at(row, lo, spot(d), core) for d in (1, -1, 2, -2)}
@@ -79,7 +91,7 @@
         copy.start()
 
     barrier = pltpu.get_barrier_semaphore()
-    partners = [partner, sibling, near_before, near_after, queries_to, queries_from, *along_z.values()]
+    partners = [partner, sibling, near_before, near_after, far_before, far_after, queries_to, queries_from, *along_z.values()]
     for device in partners:
         pl.semaphore_signal(barrier, inc=1, device_id=device, device_id_type=MESH)
 
@@ -135,6 +147,8 @@
     far_to = tuple(jnp.where(core == 0, p, n) for p, n in zip(partner, near_before))
 
     def far_copy(e):
+        if e in DIRECT:
+            return remote(block(0, e), block(3, e), far_send.at[e], line_recv.at[3, e], far_before)
         return remote(block(1 + core, e), block(3, e), far_send.at[e], line_recv.at[3, e], far_to)
 
     def sib_copy(part, e, core_=None):
@@ -164,13 +178,16 @@
         if e not in (1, 2):
             partner_copy(e).start()
             near_copy(e).start()
+            if e in DIRECT:
+                far_copy(e).start()
         sib_copy(0, e).start()
 
     def pass_far(e):
         arrived(1, e)
         if e not in (1, 2):
             arrived(2, e)
-            far_copy(e).start()
+            if e not in DIRECT:
+                far_copy(e).start()
         if e == 0:
             column_copy(0).start()
             column_copy(1).start()
@@ -202,10 +219,9 @@
     pass_far(0)
     pass_on(1)
     pass_on(2)
-    need(((0, 0), (0, 1), (1, 0)))
 
     def attend(which, spots):
-        parts = [blocks.at[c, zz, j] for zz, j in spots for c in range(2)]
+        parts = [blocks.at[c, zz, j] for c, zz, j in spots]
         count = len(parts)
         keys = jnp.concatenate([part[0:HD, :] for part in parts], axis=1)
         values = jnp.concatenate([part[HD : 2 * HD, :] for part in parts], axis=0)
@@ -253,29 +269,31 @@
         elif i == 2:
             pass_far(1)
             pass_far(2)
-            need(((0, 2), (2, 0), (1, 1), (1, 2), (0, 3), (0, 4)))
+            need(((0, 0), (0, 1), (1, 0)))
         elif i == 3:
             pass_on(5)
             pass_on(6)
             pass_last(1)
             pass_last(2)
+        elif i == 4:
             pass_far(3)
             pass_far(4)
-        elif i == 4:
             pass_on(7)
-            need(((2, 1), (2, 2), (1, 3), (1, 4), (0, 5), (0, 6)))
+            need(((0, 2), (2, 0), (1, 1), (1, 2), (0, 3), (0, 4)))
         elif i == 5:
             pass_far(5)
             pass_far(6)
+        elif i == 6:
             pass_far(7)
             pass_last(3)
             pass_last(4)
-        elif i == 6:
-            need(((2, 3), (2, 4), (1, 5), (1, 6), (0, 7), (1, 7)))
+            need(((2, 1), (2, 2), (1, 3), (1, 4), (0, 5), (0, 6)))
+        elif i == 7:
             pass_last(5)
             pass_last(6)
             pass_last(7)
-        elif i == 7:
+            need(((2, 3), (2, 4), (1, 5), (1, 6), (0, 7), (1, 7)))
+        elif i == 8:
             need(((2, 7), (2, 5), (2, 6)))
 
     def give_back():
@@ -292,33 +310,40 @@
     def choose(index, tiles):
         found = []
         for choices in zip(*tiles):
-            line_, distance = choices[-1][0], OFFSETS[choices[-1][1]]
+            side, line_, e = choices[-1]
+            distance = OFFSETS[e]
             for n in range(len(tiles) - 1):
-                line_ = jnp.where(index == n, choices[n][0], line_)
-                distance = jnp.where(index == n, OFFSETS[choices[n][1]], distance)
-            found.append((spot(distance), line_))
+                side = jnp.where(index == n, choices[n][0], side)
+                line_ = jnp.where(index == n, choices[n][1], line_)
+                distance = jnp.where(index == n, OFFSETS[choices[n][2]], distance)
+            found.append((core + side - 2 * core * side, spot(distance), line_))
         return found
 
     def item(i, carry):
-        other = (i == 1) | (i == 2) | (i == 4) | (i == 6) | (i == 7)
+        other = (i == 1) | (i == 2) | (i == 4) | (i == 6) | (i == 7) | (i == 8)
         which = jnp.where(other, 1, 0)
-        for n in range(1, 8):
+        for n in range(1, 9):
 
             @pl.when(i == n)
             def _(n=n):
                 early(n)
 
-        small = (i < 2) | (i == 7) | (i == 9)
+        small = (i < 2) | (i == 8) | (i == 11)
+        middle = (i == 2) | (i == 3) | (i == 7) | (i == 10)
 
         @pl.when(small)
         def _():
             attend(which, choose(jnp.where(i < 2, 0, 1), SMALL))
 
-        @pl.when(jnp.logical_not(small))
+        @pl.when(middle)
         def _():
-            attend(which, choose(jnp.where(i == 8, 2, i // 2 - 1), LARGE))
-
-        @pl.when(i == 7)
+            attend(which, choose(jnp.where(i < 4, 0, 1), MIDDLE))
+
+        @pl.when(jnp.logical_not(small | middle))
+        def _():
+            attend(which, choose(jnp.where(i < 6, 0, 1), LARGE))
+
+        @pl.when(i == 8)
         def _():
             give_back()
 

time: 54.5 us -> 54.1 us (level)
  no operation moved by 1% of the time
where the time goes in v3:
time: 54.1 us; the launch traced here: 54 us
  Pallas kernels  51.1 us (94%)
  local copies, waits for them, and re-layouts  2.27 us (4%)
  between operations  0.65 us (1%)
    pallas_call x1, Pallas kernels, local(): pl.pallas_call(kernel, out_shape=(jax.ShapeDtypeStruct((TOK, HEADS * HD),...  51.1 us
    unnamed x4, local copies, waits for them, and re-layouts  2.27 us

profile of v3, /device:TPU:1, one launch (start us, length us, event | category | flops | bytes accessed | tf_op | source)
XLA Modules:
  0.0 54.0 jit_solution(13574217898585992396)
XLA Ops:
  0.6 51.1 %shard_map.59 = (bf16[128,1024]{1,0:T(8,128)(2,1)}, f32[8,128]{1,0:T(8,128)}) custom-call(bf16[128,1024]{1,0:T(8,128)(2,1)} %q_hbm.1, bf16[128,128]{1,0:T(8,128)(2,1)} %k_hbm.1, bf16[128,128]{1,0:T(8,128)(2,1)} %v_hbm.1, s32[1,128]{1,0:T(1,128)} %bitcast.1), custom_call_target="tpu_custom_call" | custom-call | tf_op jit(solution)/shard_map/pallas_call | solution.py:393
  51.7 0.0 copy-start
  51.7 1.7 %copy.8 = bf16[128,1024]{1,0:T(8,128)(2,1)} copy(bf16[128,1024]{1,0:T(8,128)(2,1)} %get-tuple-element.4) | data formatting | bytes 524288
  53.4 0.0 copy-done
  53.4 0.6 %copy.9 = f32[8,128]{1,0:T(8,128)} copy(f32[8,128]{1,0:T(8,128)S(1)} %copy-done) | data formatting | bytes 8192
Async XLA Ops:
  51.7 1.7 %copy-start = (f32[8,128]{1,0:T(8,128)S(1)}, f32[8,128]{1,0:T(8,128)}, u32[]{:S(2)}) copy-start(f32[8,128]{1,0:T(8,128)} %get-tuple-element.5) | copy-start | bytes 12292
